TPU v7x, 32 devices: a whole 2x2x4 slice. The times are simulated.
32 devices in a mesh: ctx: 16 (over z, x, core), head: 2 (over y).
Axes of the slice: x: 2, y: 2, z: 4, core: 2. Of those that a mesh axis runs over, the one named last changes fastest.
Arguments:
- query_rows: bfloat16 [3072, 8192], P('ctx', 'head'), may hold values from -6 to 6
- key_rows: bfloat16 [3072, 1024], P('ctx', 'head'), may hold values from -6 to 6
- value_rows: bfloat16 [3072, 1024], P('ctx', 'head'), may hold values from -6 to 6
- attn_output: bfloat16 [3072, 8192], P('ctx', 'head'), may hold values from -6 to 6
- log_norms: float32 [64, 3072], P('head', 'ctx'), may hold values from 3 to 5
- grad_output: bfloat16 [3072, 8192], P(('ctx', 'head')), may hold values from -2.390625 to 2.390625
- span_order: int32 [32], replicated, may hold values from 0 to 31, each once
Outputs:
- grad_query: bfloat16 [3072, 8192], P(('ctx', 'head'))
- grad_key: bfloat16 [3072, 1024], P('ctx', 'head')
- grad_value: bfloat16 [3072, 1024], P('ctx', 'head')
Inputs may be any that keep to these rules, and one draw needn't show every extreme that they name: span_order is a permutation: each of the 32 spans of 96 positions is held by exactly one slot.
All inputs are finite; a program needn't handle non-finite values.
Results may differ from a plain program's by a relative error of at most 0.0051.
Values may be sent and summed in bfloat16 or wider, within the bound.
A program may use at most 192 MiB of HBM per device.

v0:
```python
import functools
import math

import jax
import jax.numpy as jnp
from jax import lax
from jax.experimental import pallas as pl
from jax.experimental.pallas import tpu as pltpu
from jax.sharding import PartitionSpec as P

QH = 64
KVH = 8
HD = 128
GROUPS = QH // KVH
KEYS = 256
LOG2E = math.log2(math.e)


def attend_kernel(
    slot_of_ref, my_span_ref,
    q_ref, d_ref, k_ref, v_ref, lse_ref, delta_ref, base_ref,
    dq_ref, dk_ref, dv_ref,
    ks, kt, vs, qs, qt, ds_rows, dt, dqt, dk_acc, dv_acc,
):
    span = base_ref.shape[1] // GROUPS
    seq = k_ref.shape[0]
    slots = q_ref.shape[0] // span
    inv_root = HD ** -0.5

    def place(p, _):
        src = pl.ds(pl.multiple_of(slot_of_ref[p] * span, span), span)
        dst = pl.ds(pl.multiple_of(p * span, span), span)
        ks[dst, :] = k_ref[src, :]
        vs[dst, :] = v_ref[src, :]
        return 0

    lax.fori_loop(0, seq // span, place, 0)

    def turn(c, _):
        rows = pl.ds(pl.multiple_of(c * KEYS, KEYS), KEYS)
        kt[c] = ks[rows, :].T
        dk_acc[rows, :] = jnp.zeros((KEYS, HD), jnp.float32)
        dv_acc[rows, :] = jnp.zeros((KEYS, HD), jnp.float32)
        return 0

    lax.fori_loop(0, seq // KEYS, turn, 0)

    def one_slot(s, _):
        rows = pl.ds(pl.multiple_of(s * span, span), span)
        for g in range(GROUPS):
            part = slice(g * span, (g + 1) * span)
            cols = slice(g * HD, (g + 1) * HD)
            qs[part, :] = q_ref[rows, cols]
            ds_rows[part, :] = d_ref[rows, cols]
        qt[...] = qs[...].T
        dt[...] = ds_rows[...].T
        dqt[...] = jnp.zeros_like(dqt)
        my_span = my_span_ref[s]

        def block(c, masked, size=1):
            wide = qt.shape[1]
            cuts = [slice(j, min(j + KEYS, wide)) for j in range(0, wide, KEYS)]
            tiles = [(i, cut) for i in range(size) for cut in cuts]

            def keys_of(i):
                return pl.ds(pl.multiple_of((c + i) * KEYS, KEYS), KEYS)

            def products(i, cut):
                scores = jnp.dot(ks[keys_of(i), :], qt[:, cut], preferred_element_type=jnp.float32)
                dprob = jnp.dot(vs[keys_of(i), :], dt[:, cut], preferred_element_type=jnp.float32)
                return scores, dprob

            probs, dscores = [], []
            ahead = products(*tiles[0])
            for n, (i, cut) in enumerate(tiles):
                scores, dprob = ahead
                if n + 1 < len(tiles):
                    ahead = products(*tiles[n + 1])
                prob = jnp.exp2(scores * (inv_root * LOG2E) - lse_ref[0, s][:, cut])
                if masked:
                    key_pos = (c + i) * KEYS + lax.broadcasted_iota(jnp.int32, prob.shape, 0)
                    prob = jnp.where(my_span * span + base_ref[:, cut] >= key_pos, prob, 0.0)
                dscores.append((prob * (dprob - delta_ref[0, s][:, cut])).astype(jnp.bfloat16))
                probs.append(prob.astype(jnp.bfloat16))
                if cut is cuts[-1]:
                    prob_low = jnp.concatenate(probs[-len(cuts):], axis=1)
                    dscore = jnp.concatenate(dscores[-len(cuts):], axis=1)
                    dv_acc[keys_of(i), :] += jnp.dot(
                        prob_low, ds_rows[...], preferred_element_type=jnp.float32
                    )
                    dk_acc[keys_of(i), :] += jnp.dot(
                        dscore, qs[...], preferred_element_type=jnp.float32
                    )
                    dqt[...] += jnp.dot(kt[c + i], dscore, preferred_element_type=jnp.float32)

        whole = (my_span * span) // KEYS
        last = (my_span * span + span + KEYS - 1) // KEYS
        lax.fori_loop(0, whole // 2, lambda c, _: (block(2 * c, False, 2), 0)[1], 0)

        @pl.when(whole % 2 == 1)
        def _():
            block(whole - 1, False)

        lax.fori_loop(whole, last, lambda c, _: (block(c, True), 0)[1], 0)

        dq = (dqt[...].T * inv_root).astype(jnp.bfloat16)
        for g in range(GROUPS):
            dq_ref[rows, g * HD:(g + 1) * HD] = dq[g * span:(g + 1) * span, :]
        return 0

    lax.fori_loop(0, slots, one_slot, 0)

    def back(p, _):
        dst = pl.ds(pl.multiple_of(slot_of_ref[p] * span, span), span)
        src = pl.ds(pl.multiple_of(p * span, span), span)
        dk_ref[dst, :] = (dk_acc[src, :] * inv_root).astype(dk_ref.dtype)
        dv_ref[dst, :] = dv_acc[src, :].astype(dv_ref.dtype)
        return 0

    lax.fori_loop(0, seq // span, back, 0)


def attend(slot_of, my_spans, q, d, k, v, lse, delta, span, part_type):
    rows = q.shape[0]
    seq = k.shape[0]
    kv_heads = k.shape[1] // HD
    slots = rows // span
    wide = GROUPS * span
    base = jnp.tile(jnp.arange(span, dtype=jnp.int32), GROUPS)[None, :]
    pairs = kv_heads * wide * seq * slots

    def by_head(height, width):
        return pl.BlockSpec((height, width), lambda h, *_: (0, h))

    row_terms = pl.BlockSpec((1, slots, 1, wide), lambda h, *_: (h, 0, 0, 0))
    return pl.pallas_call(
        attend_kernel,
        grid_spec=pltpu.PrefetchScalarGridSpec(
            num_scalar_prefetch=2,
            grid=(kv_heads,),
            in_specs=[
                by_head(rows, GROUPS * HD), by_head(rows, GROUPS * HD),
                by_head(seq, HD), by_head(seq, HD),
                row_terms, row_terms,
                pl.BlockSpec((1, wide), lambda h, *_: (0, 0)),
            ],
            out_specs=[by_head(rows, GROUPS * HD), by_head(seq, HD), by_head(seq, HD)],
            scratch_shapes=[
                pltpu.VMEM((seq, HD), jnp.bfloat16),
                pltpu.VMEM((seq // KEYS, HD, KEYS), jnp.bfloat16),
                pltpu.VMEM((seq, HD), jnp.bfloat16),
                pltpu.VMEM((wide, HD), jnp.bfloat16),
                pltpu.VMEM((HD, wide), jnp.bfloat16),
                pltpu.VMEM((wide, HD), jnp.bfloat16),
                pltpu.VMEM((HD, wide), jnp.bfloat16),
                pltpu.VMEM((HD, wide), jnp.float32),
                pltpu.VMEM((seq, HD), jnp.float32),
                pltpu.VMEM((seq, HD), jnp.float32),
            ],
        ),
        out_shape=[
            jax.ShapeDtypeStruct(q.shape, jnp.bfloat16),
            jax.ShapeDtypeStruct(k.shape, part_type),
            jax.ShapeDtypeStruct(k.shape, part_type),
        ],
        compiler_params=pltpu.CompilerParams(vmem_limit_bytes=48 * 2**20),
        cost_estimate=pl.CostEstimate(
            flops=7 * pairs * HD, bytes_accessed=2**24, transcendentals=pairs // 2
        ),
        name="attend",
    )(slot_of, my_spans, q, d, k, v, lse, delta, base)


MESH = pl.DeviceIdType.MESH
NX = 2


def place_of():
    me = lax.axis_index("ctx")
    return me // (2 * NX), (me // 2) % NX, me % 2, lax.axis_index("head")


def device_at(z, x, core, y):
    return ((z * NX + x) * 2 + core, y)


def greet(nz, ny):
    z, x, core, y = place_of()
    barrier = pltpu.get_barrier_semaphore()

    def hello(device):
        pl.semaphore_signal(barrier, inc=1, device_id=device, device_id_type=MESH)

    for dy in range(ny):
        for dc in range(2):
            if dy or dc:
                hello(device_at(z, x, (core + dc) % 2, (y + dy) % ny))
    hello(device_at(z, 1 - x, core, y))

    @pl.when(z > 0)
    def _():
        hello(device_at(z - 1, x, core, y))

    @pl.when(z < nz - 1)
    def _():
        hello(device_at(z + 1, x, core, y))

    @pl.when((z == 0) | (z == nz - 1))
    def _():
        pl.semaphore_wait(barrier, 2 * ny + 1)

    @pl.when((z > 0) & (z < nz - 1))
    def _():
        pl.semaphore_wait(barrier, 2 * ny + 2)


def remote(src, dst, sems, index, device):
    return pltpu.make_async_remote_copy(
        src_ref=src, dst_ref=dst, send_sem=sems.at[(0, *index)], recv_sem=sems.at[(1, *index)],
        device_id=device, device_id_type=MESH,
    )


def aligned(index, size):
    return pl.ds(pl.multiple_of(index * size, size), size)


def spread_kernel(
    nz, ny, q_in, o_in, k_in, v_in, d_in, l_in, q_out, o_out, k_out, v_out, d_out, l_out,
    pair_sems, group_sems, up_sems, down_sems, side_sems,
):
    z, x, core, y = place_of()
    other = 1 - core
    own = k_in.shape[0]
    rows = 2 * own
    share = d_in.shape[0]
    sibling = device_at(z, x, other, y)
    greet(nz, ny)

    chip_row = (z * NX + x) * rows
    mine = pl.ds(pl.multiple_of(chip_row + core * own, own), own)
    pairs, keeps = [], []
    for n, (src, dst, where) in enumerate((
        (k_in, k_out, mine), (v_in, v_out, mine),
        (q_in, q_out, aligned(core, own)), (o_in, o_out, aligned(core, own)),
    )):
        width = dst.shape[1]
        pairs.append(remote(
            src.at[:, aligned(other, width)], dst.at[where, :], pair_sems, (n,), sibling
        ))
        keeps.append((dst, where, src, aligned(core, width)))
    width = d_out.shape[1]
    group = []
    d_rows = aligned(core * ny + y, share)
    for dy in range(ny):
        for dc in range(2):
            yy, cc = (y + dy) % ny, (core + dc) % 2
            columns = aligned(yy * 2 + cc, width)
            if dy or dc:
                group.append(remote(
                    d_in.at[:, columns], d_out.at[d_rows, :], group_sems, (dy, dc),
                    device_at(z, x, cc, yy),
                ))
            else:
                keeps.append((d_out, d_rows, d_in, columns))
    heads = l_out.shape[1]
    pairs.append(remote(l_in.at[aligned(other, heads), :], l_out.at[core], pair_sems, (4,), sibling))

    def keep(n):
        dst, where, src, columns = keeps[n]
        dst[where, :] = src[:, columns]

    for n in range(2):
        pairs[n].start()
        keep(n)
    for n in range(2):
        pairs[n].wait_recv()

    def hop(n, zz, sems, device):
        ref = (k_out, v_out)[n].at[aligned(zz * NX + x, rows), :]
        return remote(ref, ref, sems, (n, zz), device)

    def up(n, zz):
        return hop(n, zz, up_sems, device_at(z + 1, x, core, y))

    def down(n, zz):
        return hop(n, zz, down_sems, device_at(z - 1, x, core, y))

    def side(n, zz):
        return hop(n, zz, side_sems, device_at(z, 1 - x, core, y))

    def side_in(n, zz):
        ref = (k_out, v_out)[n].at[aligned(zz * NX + 1 - x, rows), :]
        return remote(ref, ref, side_sems, (n, zz), device_at(z, 1 - x, core, y))

    for n in range(2):
        @pl.when(z < nz - 1)
        def _():
            up(n, z).start()

        @pl.when(z > 0)
        def _():
            down(n, z).start()

        side(n, z).start()
    for copy in reversed(group):
        copy.start()
    for n in range(2, 5):
        pairs[n].start()
        keep(n)
    l_out[core] = l_in[aligned(core, heads), :]

    for step in range(1, nz):
        for n in range(2):
            @pl.when(z - step >= 0)
            def _():
                up(n, z - step).wait_recv()

                @pl.when(z < nz - 1)
                def _():
                    up(n, z - step).start()

                side(n, z - step).start()

            @pl.when(z + step < nz)
            def _():
                down(n, z + step).wait_recv()

                @pl.when(z > 0)
                def _():
                    down(n, z + step).start()

                side(n, z + step).start()

    for n in range(2):
        for zz in range(nz):
            side_in(n, zz).wait_recv()
            side(n, zz).wait_send()

            @pl.when((zz <= z) & (z < nz - 1))
            def _():
                up(n, zz).wait_send()

            @pl.when((zz >= z) & (z > 0))
            def _():
                down(n, zz).wait_send()

        pairs[n].wait_send()
        pairs[n + 2].wait()
    pairs[4].wait()
    for copy in group:
        copy.wait()


def spread(q, o, k, v, d, lse, ctx, ny):
    nz = ctx // (2 * NX)
    rows = 2 * q.shape[0]
    seq = k.shape[0] * ctx

    def like(height, x, parts):
        return jax.ShapeDtypeStruct((height, x.shape[1] // parts), x.dtype)

    whole = pl.BlockSpec(memory_space=pltpu.VMEM)
    dma = pltpu.SemaphoreType.DMA
    return pl.pallas_call(
        functools.partial(spread_kernel, nz, ny),
        out_shape=[like(rows, q, 2), like(rows, o, 2), like(seq, k, 2), like(seq, v, 2),
                   like(rows, d, 2 * ny),
                   jax.ShapeDtypeStruct((2, lse.shape[0] // 2, lse.shape[1]), lse.dtype)],
        in_specs=[whole] * 6,
        out_specs=[whole] * 6,
        scratch_shapes=[
            dma((2, 5)), dma((2, ny, 2)), dma((2, 2, nz)), dma((2, 2, nz)), dma((2, 2, nz)),
        ],
        compiler_params=pltpu.CompilerParams(
            collective_id=0, has_side_effects=True, vmem_limit_bytes=40 * 2**20
        ),
        name="spread",
    )(q, o, k, v, d, lse)


def fold_kernel(
    nz, ny, dk_in, dv_in, dq_in, gk_out, gv_out, gq_out,
    side_buf, up_buf, down_buf, out_buf, fin,
    local_sems, pair_sems, group_sems, up_sems, down_sems, side_sems,
):
    z, x, core, y = place_of()
    other = 1 - core
    rows = fin.shape[1]
    own = rows // 2
    share = gq_out.shape[0]
    parts = (dk_in, dv_in)
    greet(nz, ny)

    def side(n, zz):
        return remote(
            parts[n].at[aligned(zz * NX + 1 - x, rows), :], side_buf.at[n, zz], side_sems, (n, zz),
            device_at(z, 1 - x, core, y),
        )

    def up(n, zz):
        return remote(
            out_buf.at[n, zz], up_buf.at[n, zz], up_sems, (n, zz), device_at(z + 1, x, core, y)
        )

    def down(n, zz):
        return remote(
            out_buf.at[n, zz], down_buf.at[n, zz], down_sems, (n, zz), device_at(z - 1, x, core, y)
        )

    order = []
    for far in range(nz // 2):
        order.append(jnp.where(z < nz // 2, nz - 1 - far, far))
        order.append(jnp.where(z < nz // 2, far, nz - 1 - far))

    width = dq_in.shape[1]
    group = []
    for dy in range(ny):
        for dc in range(2):
            yy, cc = (y + dy) % ny, (core + dc) % 2
            src = dq_in.at[aligned(cc * ny + yy, share), :]
            dst = gq_out.at[:, aligned(y * 2 + core, width)]
            if dy or dc:
                group.append(remote(src, dst, group_sems, (dy, dc), device_at(z, x, cc, yy)))
            else:
                keep = pltpu.make_async_copy(src, dst, local_sems.at[2])
    for zz in order:
        for n in range(2):
            side(n, zz).start()
    for copy in reversed(group):
        copy.start()
    keep.start()

    def total(n, zz):
        mine = parts[n][aligned(zz * NX + x, rows), :].astype(jnp.float32)
        return mine + side_buf[n, zz].astype(jnp.float32)

    for zz in order:
        for n in range(2):
            @pl.when(zz > z)
            def _():
                side(n, zz).wait_recv()

                @pl.when(z == 0)
                def _():
                    out_buf[n, zz] = total(n, zz).astype(jnp.bfloat16)

                @pl.when(z > 0)
                def _():
                    up(n, zz).wait_recv()
                    out_buf[n, zz] = (
                        total(n, zz) + up_buf[n, zz].astype(jnp.float32)
                    ).astype(jnp.bfloat16)

                up(n, zz).start()

            @pl.when(zz < z)
            def _():
                side(n, zz).wait_recv()

                @pl.when(z == nz - 1)
                def _():
                    out_buf[n, zz] = total(n, zz).astype(jnp.bfloat16)

                @pl.when(z < nz - 1)
                def _():
                    down(n, zz).wait_recv()
                    out_buf[n, zz] = (
                        total(n, zz) + down_buf[n, zz].astype(jnp.float32)
                    ).astype(jnp.bfloat16)

                down(n, zz).start()

    ends = []
    for n, out in enumerate((gk_out, gv_out)):
        side(n, z).wait_recv()

        @pl.when(z == 0)
        def _():
            down(n, z).wait_recv()
            fin[n] = (total(n, z) + down_buf[n, z].astype(jnp.float32)).astype(jnp.bfloat16)

        @pl.when(z == nz - 1)
        def _():
            up(n, z).wait_recv()
            fin[n] = (total(n, z) + up_buf[n, z].astype(jnp.float32)).astype(jnp.bfloat16)

        @pl.when((z > 0) & (z < nz - 1))
        def _():
            up(n, z).wait_recv()
            down(n, z).wait_recv()
            fin[n] = (
                total(n, z) + up_buf[n, z].astype(jnp.float32) + down_buf[n, z].astype(jnp.float32)
            ).astype(jnp.bfloat16)

        columns = aligned(core, fin.shape[2])
        pair = remote(
            fin.at[n, aligned(other, own), :], out.at[:, columns], pair_sems, (n,),
            device_at(z, x, other, y),
        )
        here = pltpu.make_async_copy(
            fin.at[n, aligned(core, own), :], out.at[:, columns], local_sems.at[n]
        )
        pair.start()
        here.start()
        ends += [pair, here]

    for copy in ends + group + [keep]:
        copy.wait()
    for n in range(2):
        for zz in range(nz):
            side(n, zz).wait_send()

            @pl.when(zz > z)
            def _():
                up(n, zz).wait_send()

            @pl.when(zz < z)
            def _():
                down(n, zz).wait_send()


def fold(dk, dv, dq, ctx, ny):
    nz = ctx // (2 * NX)
    rows = dq.shape[0]
    own = rows // 2
    width = dk.shape[1]
    anywhere = pl.BlockSpec(memory_space=pl.ANY)
    whole = pl.BlockSpec(memory_space=pltpu.VMEM)
    dma = pltpu.SemaphoreType.DMA
    buffers = pltpu.VMEM((2, nz, rows, width), jnp.bfloat16)
    kv_out = jax.ShapeDtypeStruct((own, 2 * width), jnp.bfloat16)
    return pl.pallas_call(
        functools.partial(fold_kernel, nz, ny),
        out_shape=[kv_out, kv_out,
                   jax.ShapeDtypeStruct((rows // (2 * ny), dq.shape[1] * 2 * ny), jnp.bfloat16)],
        in_specs=[whole, whole, anywhere],
        out_specs=[anywhere] * 3,
        scratch_shapes=[
            buffers, buffers, buffers, buffers, pltpu.VMEM((2, rows, width), jnp.bfloat16),
            dma((3,)), dma((2, 2)), dma((2, ny, 2)), dma((2, 2, nz)), dma((2, 2, nz)), dma((2, 2, nz)),
        ],
        compiler_params=pltpu.CompilerParams(
            collective_id=1, has_side_effects=True, vmem_limit_bytes=32 * 2**20
        ),
        name="fold",
    )(dk, dv, dq)


def row_terms_of(terms, kv_heads, span):
    rows = terms.shape[1]
    cut = terms.reshape(kv_heads, GROUPS, rows // span, span)
    return cut.transpose(0, 2, 1, 3).reshape(kv_heads, rows // span, 1, GROUPS * span)


def per_device(query_rows, key_rows, value_rows, attn_output, log_norms, grad_output, span_order):
    own_rows = query_rows.shape[0]
    span = own_rows // 2
    ctx = lax.axis_size("ctx")
    me = lax.axis_index("ctx")
    cores = 2 if (key_rows.shape[1] // HD) % 2 == 0 and ctx % 2 == 0 else 1
    chip_groups = [[i * cores + c for c in range(cores)] for i in range(ctx // cores)]
    ring_groups = [[i * cores + c for i in range(ctx // cores)] for c in range(cores)]

    def to_heads(x, split=1, concat=0):
        if cores == 1:
            return x
        return lax.all_to_all(
            x, "ctx", split_axis=split, concat_axis=concat, axis_index_groups=chip_groups, tiled=True
        )

    ny = lax.axis_size("head")
    by_kernels = cores == 2 and ctx % (4 * NX) == 0
    if by_kernels:
        q, o, k, v, d, lse = spread(
            query_rows, attn_output, key_rows, value_rows, grad_output, log_norms, ctx, ny
        )
        lse = jnp.concatenate([lse[0], lse[1]], axis=1)
    else:
        lse = to_heads(log_norms, 0, 1)
        q = to_heads(query_rows)
        o = to_heads(attn_output)
        d = to_heads(lax.all_to_all(grad_output, "head", split_axis=1, concat_axis=0, tiled=True))
        kv = jnp.concatenate([to_heads(key_rows), to_heads(value_rows)], axis=1)
        kv = lax.all_gather(kv, "ctx", axis=0, axis_index_groups=ring_groups, tiled=True)
        k, v = kv[:, :kv.shape[1] // 2], kv[:, kv.shape[1] // 2:]
    half = k.shape[1]
    kv_heads = half // HD
    rows = q.shape[0]
    delta = jnp.sum(
        (d.astype(jnp.float32) * o.astype(jnp.float32)).reshape(rows, kv_heads * GROUPS, HD), axis=-1
    ).T
    spans = span_order.shape[0]
    slots = rows // span
    ids = jnp.arange(spans, dtype=jnp.int32)
    slot_of = jnp.sum(jnp.where(span_order[None, :] == ids[:, None], ids[None, :], 0), axis=1)
    my_spans = lax.dynamic_slice_in_dim(span_order, (me // cores) * slots, slots)
    dq, dk, dv = attend(
        slot_of, my_spans, q, d, k, v,
        row_terms_of(lse * LOG2E, kv_heads, span), row_terms_of(delta, kv_heads, span),
        span, jnp.bfloat16 if by_kernels else jnp.float32,
    )
    if by_kernels:
        grad_key, grad_value, grad_query = fold(dk, dv, dq, ctx, ny)
        return (grad_query, grad_key, grad_value)
    dkv = jnp.concatenate([dk, dv], axis=1)
    dkv = lax.psum_scatter(dkv, "ctx", scatter_dimension=0, axis_index_groups=ring_groups, tiled=True)
    dkv = dkv.astype(jnp.bfloat16)
    grad_key = to_heads(dkv[:, :half], 0, 1)
    grad_value = to_heads(dkv[:, half:], 0, 1)
    dq = to_heads(dq, 0, 1)
    grad_query = lax.all_to_all(dq, "head", split_axis=0, concat_axis=1, tiled=True)
    return (grad_query, grad_key, grad_value)


def solution(mesh):
    return jax.shard_map(
        per_device,
        mesh=mesh,
        in_specs=(
            P("ctx", "head"),
            P("ctx", "head"),
            P("ctx", "head"),
            P("ctx", "head"),
            P("head", "ctx"),
            P(("ctx", "head"), None),
            P(),
        ),
        out_specs=(P(("ctx", "head"), None), P("ctx", "head"), P("ctx", "head")),
        check_vma=False,
    )
```

profile of v0, /device:TPU:9, one launch (start us, length us, event | category | flops | bytes accessed | tf_op | source)
XLA Modules:
  0.0 152.6 jit_solution(13178889940243386604)
XLA Ops:
  0.6 0.7 dynamic_slice.3.my_span_ref
  1.4 0.0 copy-start
  1.4 1.4 copy-done
  2.8 0.0 copy-start.1
  2.8 1.4 copy-done.1
  4.2 0.0 copy-start.2
  4.2 1.4 copy-done.2
  5.6 0.0 copy-start.4
  5.6 0.9 copy-done.4
  6.5 0.0 copy-start.5
  6.5 0.9 copy-done.5
  7.5 0.0 copy-start.6
  7.5 0.8 copy-done.6
  8.2 39.7 %spread.1 = (bf16[384,2048]{1,0:T(8,128)(2,1)S(1)}, bf16[384,2048]{1,0:T(8,128)(2,1)S(1)}, bf16[3072,256]{1,0:T(8,128)(2,1)S(1)}, bf16[3072,256]{1,0:T(8,128)(2,...) custom-call(bf16[192,4096]{1,0:T(8,128)(2,1)S(1)} %copy-done, bf16[192,4096]{1,0:T(8,128)(2,1)S(1)} %copy-done.1, ...), custom_call_target="tpu_custom_call" | custom-call | tf_op jit(solution)/shard_map/spread/pallas_call | solution.py:365
  47.9 0.0 copy-start.7
  47.9 1.1 copy-done.7
  49.1 0.0 copy-start.8
  49.1 1.2 copy-done.8
  50.2 0.0 copy-start.9
  50.2 1.1 copy-done.9
  51.4 0.0 copy-start.3
  51.4 0.1 maximum_multiply_fusion
  51.4 0.1 mul.19
  51.5 0.1 reshape.23.lse_ref
  51.7 0.6 multiply_bitcast_fusion
  52.3 0.3 copy-done.3
  52.6 2.3 %copy.19 = f32[48,8,16,128]{3,2,1,0:T(8,128)} copy(f32[48,8,16,128]{3,1,2,0:T(8,128)S(1)} %multiply_bitcast_fusion) | data formatting | bytes 6291456
  54.8 0.0 copy-start.10
  54.8 2.8 %reduce_sum.19 = f32[384,16]{1,0:T(8,128)S(1)} reduce(f32[384,16,128]{2,1,0:T(8,128)} %bitcast.16, f32[]{:T(128)} %constant.28.clone.1), dimensions={2}, to_apply=%region_1.2 | reduce | flops 780288 | bytes 3170308 | tf_op jit(solution)/shard_map/reduce_sum | solution.py:590
  57.6 0.1 copy.17
  57.7 0.1 reshape.25
  57.8 0.1 reshape.26.delta_ref
  57.9 0.1 broadcast_in_dim_tile.3.base_ref
  58.0 0.0 copy-done.10
  58.0 0.1 select_reduce_fusion.slot_of_ref
  58.1 38.7 %attend.1 = (bf16[384,2048]{1,0:T(8,128)(2,1)S(1)}, bf16[3072,256]{1,0:T(8,128)(2,1)S(1)}, bf16[3072,256]{1,0:T(8,128)(2,1)S(1)}) custom-call(s32[32]{0:T(128)S(1)} %select_reduce_fusion.slot_of_ref, s32[4]{0:T(128)S(1)} %dynamic_slice.3.my_span_ref, bf16[384,2048]{1,0:T(8,128)(2,1)} %copy-done.7, bf16[384,2048]{1,0:T(8,128)(2,1)} %copy-done.3, ...), custom_call_target="tpu_custom_call" | custom-call | flops 16911433728 | bytes 16777216 | tf_op jit(solution)/shard_map/attend/pallas_call | solution.py:136
  96.9 53.2 %fold.1 = (bf16[192,512]{1,0:T(8,128)(2,1)S(1)}, bf16[192,512]{1,0:T(8,128)(2,1)S(1)}, bf16[96,8192]{1,0:T(8,128)(2,1)S(1)}) custom-call(bf16[3072,256]{1,0:T(8,128)(2,1)S(1)} %get-tuple-element.21.dk_in, bf16[3072,256]{1,0:T(8,128)(2,1)S(1)} %get-tuple-element.22.dv_in, bf16[384,2048]{1,0:T(8,128)(2,1)S(1)} %get-tuple-element.23.dq_in), custom_call_target="tpu_custom_call" | custom-call | tf_op jit(solution)/shard_map/fold/pallas_call | solution.py:533
  150.1 1.1 copy.25
  151.3 0.7 copy.26
  152.0 0.7 copy.27
  (4 shorter events, 0.0 us)
Async XLA Ops:
  1.4 1.4 copy-start
  2.8 1.4 copy-start.1
  4.2 1.4 copy-start.2
  5.6 0.9 copy-start.4
  6.5 0.9 copy-start.5
  7.5 0.8 copy-start.6
  47.9 1.1 copy-start.7
  49.1 1.2 copy-start.8
  50.2 1.1 copy-start.9
  51.4 1.2 copy-start.3
  54.8 3.2 %copy-start.10 = (s32[32]{0:T(128)S(1)}, s32[32]{0:T(128)}, u32[]{:S(2)}) copy-start(s32[32]{0:T(128)} %param.13) | copy-start | bytes 388
where the time goes:
time: 155 us; the launch traced here: 153 us
  Pallas kernels  132 us (85%)
  local copies, waits for them, and re-layouts  16.6 us (11%)
  other arithmetic  3.58 us (2%)
    pallas_call x1, Pallas kernels, fold(): pl.pallas_call(functools.partial(fold_kernel, nz, ny), out_shape=[kv_out,...  53.2 us
    pallas_call x1, Pallas kernels, spread(): pl.pallas_call(functools.partial(spread_kernel, nz, ny), out_shape=[like(...  39.7 us
    pallas_call x1, Pallas kernels, attend(): pl.pallas_call(attend_kernel, grid_spec=pltpu.PrefetchScalarGridSpec(num_...  38.7 us
    unnamed x26, local copies, waits for them, and re-layouts  15.4 us

commit v1 on v0

--- a/solution.py
+++ b/solution.py
@@ -14,6 +14,12 @@
 GROUPS = QH // KVH
 KEYS = 256
 LOG2E = math.log2(math.e)
+
+
+def over_rows(left, right):
+    return lax.dot_general(
+        left, right, (((1,), (1,)), ((), ())), preferred_element_type=jnp.float32
+    )
 
 
 def attend_kernel(
@@ -39,8 +45,8 @@
     def turn(c, _):
         rows = pl.ds(pl.multiple_of(c * KEYS, KEYS), KEYS)
         kt[c] = ks[rows, :].T
-        dk_acc[rows, :] = jnp.zeros((KEYS, HD), jnp.float32)
-        dv_acc[rows, :] = jnp.zeros((KEYS, HD), jnp.float32)
+        dk_acc[c] = jnp.zeros((HD, KEYS), jnp.float32)
+        dv_acc[c] = jnp.zeros((HD, KEYS), jnp.float32)
         return 0
 
     lax.fori_loop(0, seq // KEYS, turn, 0)
@@ -85,12 +91,8 @@
                 if cut is cuts[-1]:
                     prob_low = jnp.concatenate(probs[-len(cuts):], axis=1)
                     dscore = jnp.concatenate(dscores[-len(cuts):], axis=1)
-                    dv_acc[keys_of(i), :] += jnp.dot(
-                        prob_low, ds_rows[...], preferred_element_type=jnp.float32
-                    )
-                    dk_acc[keys_of(i), :] += jnp.dot(
-                        dscore, qs[...], preferred_element_type=jnp.float32
-                    )
+                    dv_acc[c + i] += over_rows(dt[...], prob_low)
+                    dk_acc[c + i] += over_rows(qt[...], dscore)
                     dqt[...] += jnp.dot(kt[c + i], dscore, preferred_element_type=jnp.float32)
 
         whole = (my_span * span) // KEYS
@@ -110,11 +112,19 @@
 
     lax.fori_loop(0, slots, one_slot, 0)
 
+    def straighten(c, _):
+        rows = pl.ds(pl.multiple_of(c * KEYS, KEYS), KEYS)
+        ks[rows, :] = (dk_acc[c].T * inv_root).astype(ks.dtype)
+        vs[rows, :] = dv_acc[c].T.astype(vs.dtype)
+        return 0
+
+    lax.fori_loop(0, seq // KEYS, straighten, 0)
+
     def back(p, _):
         dst = pl.ds(pl.multiple_of(slot_of_ref[p] * span, span), span)
         src = pl.ds(pl.multiple_of(p * span, span), span)
-        dk_ref[dst, :] = (dk_acc[src, :] * inv_root).astype(dk_ref.dtype)
-        dv_ref[dst, :] = dv_acc[src, :].astype(dv_ref.dtype)
+        dk_ref[dst, :] = ks[src, :].astype(dk_ref.dtype)
+        dv_ref[dst, :] = vs[src, :].astype(dv_ref.dtype)
         return 0
 
     lax.fori_loop(0, seq // span, back, 0)
@@ -154,8 +164,8 @@
                 pltpu.VMEM((wide, HD), jnp.bfloat16),
                 pltpu.VMEM((HD, wide), jnp.bfloat16),
                 pltpu.VMEM((HD, wide), jnp.float32),
-                pltpu.VMEM((seq, HD), jnp.float32),
-                pltpu.VMEM((seq, HD), jnp.float32),
+                pltpu.VMEM((seq // KEYS, HD, KEYS), jnp.float32),
+                pltpu.VMEM((seq // KEYS, HD, KEYS), jnp.float32),
             ],
         ),
         out_shape=[
@@ -226,7 +236,8 @@
 
 
 def spread_kernel(
-    nz, ny, q_in, o_in, k_in, v_in, d_in, l_in, q_out, o_out, k_out, v_out, d_out, l_out,
+    nz, ny, q_hbm, o_hbm, k_in, v_in, d_hbm, l_in, q_hbm_out, d_hbm_out, k_out, v_out, l_out, delta_out,
+    q_in, o_in, d_in, q_out, o_out, d_out, local_sems,
     pair_sems, group_sems, up_sems, down_sems, side_sems,
 ):
     z, x, core, y = place_of()
@@ -235,6 +246,16 @@
     rows = 2 * own
     share = d_in.shape[0]
     sibling = device_at(z, x, other, y)
+    staged = [
+        pltpu.make_async_copy(src, dst, local_sems.at[n])
+        for n, (src, dst) in enumerate(((d_hbm, d_in), (q_hbm, q_in), (o_hbm, o_in)))
+    ]
+    flushed = [
+        pltpu.make_async_copy(src, dst, local_sems.at[3 + n])
+        for n, (src, dst) in enumerate(((d_out, d_hbm_out), (q_out, q_hbm_out)))
+    ]
+    for copy in staged:
+        copy.start()
     greet(nz, ny)
 
     chip_row = (z * NX + x) * rows
@@ -303,8 +324,11 @@
             down(n, z).start()
 
         side(n, z).start()
+    staged[0].wait()
     for copy in reversed(group):
         copy.start()
+    staged[1].wait()
+    staged[2].wait()
     for n in range(2, 5):
         pairs[n].start()
         keep(n)
@@ -332,6 +356,15 @@
 
                 side(n, z + step).start()
 
+    for copy in group + pairs[2:]:
+        copy.wait()
+    for copy in flushed:
+        copy.start()
+    for h in range(delta_out.shape[0]):
+        cols = slice(h * HD, (h + 1) * HD)
+        terms = d_out[:, cols].astype(jnp.float32) * o_out[:, cols].astype(jnp.float32)
+        delta_out[h:h + 1, :] = jnp.sum(terms.T, axis=0, keepdims=True)
+
     for n in range(2):
         for zz in range(nz):
             side_in(n, zz).wait_recv()
@@ -346,9 +379,7 @@
                 down(n, zz).wait_send()
 
         pairs[n].wait_send()
-        pairs[n + 2].wait()
-    pairs[4].wait()
-    for copy in group:
+    for copy in flushed:
         copy.wait()
 
 
@@ -360,16 +391,20 @@
     def like(height, x, parts):
         return jax.ShapeDtypeStruct((height, x.shape[1] // parts), x.dtype)
 
+    anywhere = pl.BlockSpec(memory_space=pl.ANY)
     whole = pl.BlockSpec(memory_space=pltpu.VMEM)
     dma = pltpu.SemaphoreType.DMA
     return pl.pallas_call(
         functools.partial(spread_kernel, nz, ny),
-        out_shape=[like(rows, q, 2), like(rows, o, 2), like(seq, k, 2), like(seq, v, 2),
-                   like(rows, d, 2 * ny),
-                   jax.ShapeDtypeStruct((2, lse.shape[0] // 2, lse.shape[1]), lse.dtype)],
-        in_specs=[whole] * 6,
-        out_specs=[whole] * 6,
+        out_shape=[like(rows, q, 2), like(rows, d, 2 * ny), like(seq, k, 2), like(seq, v, 2),
+                   jax.ShapeDtypeStruct((2, lse.shape[0] // 2, lse.shape[1]), lse.dtype),
+                   jax.ShapeDtypeStruct((lse.shape[0] // 2, rows), jnp.float32)],
+        in_specs=[anywhere, anywhere, whole, whole, anywhere, whole],
+        out_specs=[anywhere, anywhere, whole, whole, whole, whole],
         scratch_shapes=[
+            pltpu.VMEM(q.shape, q.dtype), pltpu.VMEM(o.shape, o.dtype), pltpu.VMEM(d.shape, d.dtype),
+            pltpu.VMEM((rows, q.shape[1] // 2), q.dtype), pltpu.VMEM((rows, q.shape[1] // 2), o.dtype),
+            pltpu.VMEM((rows, q.shape[1] // 2), d.dtype), dma((5,)),
             dma((2, 5)), dma((2, ny, 2)), dma((2, 2, nz)), dma((2, 2, nz)), dma((2, 2, nz)),
         ],
         compiler_params=pltpu.CompilerParams(
@@ -572,7 +607,7 @@
     ny = lax.axis_size("head")
     by_kernels = cores == 2 and ctx % (4 * NX) == 0
     if by_kernels:
-        q, o, k, v, d, lse = spread(
+        q, d, k, v, lse, delta = spread(
             query_rows, attn_output, key_rows, value_rows, grad_output, log_norms, ctx, ny
         )
         lse = jnp.concatenate([lse[0], lse[1]], axis=1)
@@ -587,9 +622,9 @@
     half = k.shape[1]
     kv_heads = half // HD
     rows = q.shape[0]
-    delta = jnp.sum(
-        (d.astype(jnp.float32) * o.astype(jnp.float32)).reshape(rows, kv_heads * GROUPS, HD), axis=-1
-    ).T
+    if not by_kernels:
+        terms = d.astype(jnp.float32) * o.astype(jnp.float32)
+        delta = jnp.sum(terms.reshape(rows, kv_heads * GROUPS, HD), axis=-1).T
     spans = span_order.shape[0]
     slots = rows // span
     ids = jnp.arange(spans, dtype=jnp.int32)

time: 155 us -> 151 us (0.974)
  other arithmetic: 3.58 us -> 0.84 us
    pallas_call x1, Pallas kernels: 38.7 us -> 44.1 us  [attend(): pl.pallas_call(attend_kernel, grid_spec=pltpu.PrefetchScalarGridSpec(num_...]
    pallas_call x1, Pallas kernels: 53.2 us -> 49.2 us  [fold(): pl.pallas_call(functools.partial(fold_kernel, nz, ny), out_shape=[kv_out,...]
    reduce_sum x1 -> x0, other arithmetic: 2.78 us -> none  [per_device(): jnp.sum((d.astype(jnp.float32) * o.astype(jnp.float32)).reshape(rows, kv_...]
    unnamed x26 -> x23, local copies, waits for them, and re-layouts: 15.4 us -> 13.9 us
where the time goes in v1:
time: 151 us; the launch traced here: 150 us
  Pallas kernels  133 us (88%)
  local copies, waits for them, and re-layouts  15.1 us (10%)
    pallas_call x1, Pallas kernels, fold(): pl.pallas_call(functools.partial(fold_kernel, nz, ny), out_shape=[kv_out,...  49.2 us
    pallas_call x1, Pallas kernels, attend(): pl.pallas_call(attend_kernel, grid_spec=pltpu.PrefetchScalarGridSpec(num_...  44.1 us
    pallas_call x1, Pallas kernels, spread(): pl.pallas_call(functools.partial(spread_kernel, nz, ny), out_shape=[like(...  40.1 us
    unnamed x23, local copies, waits for them, and re-layouts  13.9 us

profile of v1, /device:TPU:9, one launch (start us, length us, event | category | flops | bytes accessed | tf_op | source)
XLA Modules:
  0.0 150.1 jit_solution(4756579833666925932)
XLA Ops:
  0.6 0.7 dynamic_slice.3.my_span_ref
  1.4 0.8 select_reduce_fusion.slot_of_ref
  2.2 0.1 broadcast_in_dim_tile.3.base_ref
  2.2 0.0 copy-start
  2.2 1.4 copy-done
  3.6 0.0 copy-start.1
  3.7 1.4 copy-done.1
  5.1 0.0 copy-start.2
  5.1 1.4 copy-done.2
  6.5 0.0 copy-start.3
  6.5 0.9 copy-done.3
  7.4 0.0 copy-start.4
  7.4 0.9 copy-done.4
  8.3 0.0 copy-start.5
  8.3 0.8 copy-done.5
  9.1 40.1 %spread.1 = (bf16[384,2048]{1,0:T(8,128)(2,1)S(1)}, bf16[384,2048]{1,0:T(8,128)(2,1)S(1)}, bf16[3072,256]{1,0:T(8,128)(2,1)S(1)}, bf16[3072,256]{1,0:T(8,128)(2,...) custom-call(bf16[192,4096]{1,0:T(8,128)(2,1)S(1)} %copy-done, bf16[192,4096]{1,0:T(8,128)(2,1)S(1)} %copy-done.1, ...), custom_call_target="tpu_custom_call" | custom-call | tf_op jit(solution)/shard_map/spread/pallas_call | solution.py:397
  49.2 0.0 copy-start.6
  49.2 1.1 copy-done.6
  50.3 0.0 copy-start.7
  50.3 1.1 copy-done.7
  51.5 0.0 copy-start.8
  51.5 1.1 copy-done.8
  52.6 0.0 copy-start.9
  52.6 1.1 copy-done.9
  53.8 0.1 reshape.21
  53.9 0.1 reshape.22.delta_ref
  54.0 0.1 maximum_multiply_fusion
  54.1 0.1 mul.16
  54.2 0.1 reshape.20.lse_ref
  54.3 44.1 %attend.1 = (bf16[384,2048]{1,0:T(8,128)(2,1)S(1)}, bf16[3072,256]{1,0:T(8,128)(2,1)S(1)}, bf16[3072,256]{1,0:T(8,128)(2,1)S(1)}) custom-call(s32[32]{0:T(128)S(1)} %select_reduce_fusion.slot_of_ref, s32[4]{0:T(128)S(1)} %dynamic_slice.3.my_span_ref, bf16[384,2048]{1,0:T(8,128)(2,1)} %copy-done.6, bf16[384,2048]{1,0:T(8,128)(2,1)} %copy-done.7, ...), custom_call_target="tpu_custom_call" | custom-call | flops 16911433728 | bytes 16777216 | tf_op jit(solution)/shard_map/attend/pallas_call | solution.py:146
  98.4 49.2 %fold.1 = (bf16[192,512]{1,0:T(8,128)(2,1)S(1)}, bf16[192,512]{1,0:T(8,128)(2,1)S(1)}, bf16[96,8192]{1,0:T(8,128)(2,1)S(1)}) custom-call(bf16[3072,256]{1,0:T(8,128)(2,1)S(1)} %get-tuple-element.21.dk_in, bf16[3072,256]{1,0:T(8,128)(2,1)S(1)} %get-tuple-element.22.dv_in, bf16[384,2048]{1,0:T(8,128)(2,1)S(1)} %get-tuple-element.23.dq_in), custom_call_target="tpu_custom_call" | custom-call | tf_op jit(solution)/shard_map/fold/pallas_call | solution.py:568
  147.6 1.1 copy.21
  148.8 0.7 copy.22
  149.4 0.7 copy.23
  (4 shorter events, 0.0 us)
Async XLA Ops:
  2.2 1.4 copy-start
  3.6 1.4 copy-start.1
  5.1 1.4 copy-start.2
  6.5 0.9 copy-start.3
  7.4 0.9 copy-start.4
  8.3 0.8 copy-start.5
  49.2 1.1 copy-start.6
  50.3 1.2 copy-start.7
  51.5 1.2 copy-start.8
  52.6 1.1 copy-start.9
